TPU v7x, 256 devices: a whole 4x4x8 slice. The times are simulated.
256 devices in a mesh: store: 32 (over y, z), tp: 8 (over x, core).
Axes of the slice: x: 4, y: 4, z: 8, core: 2. Of those that a mesh axis runs over, the one named last changes fastest.
Arguments:
- hidden: bfloat16 [16384, 8192], P('store', 'tp'), may hold values from -6 to 6
- gain: bfloat16 [8192], replicated, may hold values from 0.099609375 to 1.8984375
- w_query: bfloat16 [8192, 4096], P('store', 'tp'), may hold values from -0.09375 to 0.09375
- key_matrix: bfloat16 [8192, 1024], P('store', 'tp'), may hold values from -0.09375 to 0.09375
- value_matrix: bfloat16 [8192, 1024], P('store', 'tp'), may hold values from -0.1875 to 0.1875
- passage_cache: bfloat16 [128, 1024, 2048], P(None, 'store', 'tp'), may hold values from -330 to 330
- passage_ids: int32 [32, 6], P('store'), may hold values from 0 to 127
- placement: int32 [128], replicated, may hold values from 0 to 31
- tile_index: int32 [32, 4], P('store'), may hold values from 0 to 47, as said below
- tile_count: int32 [32], P('store'), may hold values from 1 to 4, 64 in all
Outputs:
- attended: bfloat16 [16384, 4096], P('store', 'tp')
Inputs may be any that keep to these rules, and one draw needn't show every extreme that they name: `tile_index`: the tiles of one request are distinct. Slots from tile_count[r] on are unused; some request uses all 4.
All inputs are finite; a program needn't handle non-finite values. No bound on the sum of `tile_count` on one device may be relied on, other than what follows from the above.
Results may differ from a plain program's by a relative error of at most 0.025.
Values may be sent and summed in bfloat16 or wider, within the bound.
A program may use at most 128 MiB of HBM per device.

v0:
```python
import math

import jax
import jax.numpy as jnp
from jax import lax
from jax.sharding import PartitionSpec as P

HEAD_SIZE = 128


def rotate_pairs(vectors, positions):
    half_size = vectors.shape[-1] // 2
    exponent = jnp.arange(half_size, dtype=jnp.float32) * (2.0 / vectors.shape[-1])
    frequency = jnp.exp(-math.log(500000.0) * exponent)
    angles = positions.astype(jnp.float32)[:, None] * frequency[None, :]
    cosine = jnp.cos(angles)[:, None, :]
    sine = jnp.sin(angles)[:, None, :]
    first_half = vectors[..., :half_size]
    second_half = vectors[..., half_size:]
    return jnp.concatenate(
        [first_half * cosine - second_half * sine, second_half * cosine + first_half * sine],
        axis=-1,
    )


def attend_heads(query_rot, keys, value_rows, allowed, query_group_size):
    score_scale = 1.0 / math.sqrt(query_rot.shape[-1])

    def one_head(head_index):
        query_head = lax.dynamic_index_in_dim(query_rot, head_index, 1, keepdims=False)
        kv_index = head_index // query_group_size
        key_head = lax.dynamic_index_in_dim(keys, kv_index, 1, keepdims=False)
        value_head = lax.dynamic_index_in_dim(value_rows, kv_index, 1, keepdims=False)
        scores = (
            lax.dot_general(
                query_head, key_head, (((1,), (1,)), ((), ())), preferred_element_type=jnp.float32
            )
            * score_scale
        )
        scores = jnp.where(allowed, scores, -jnp.inf)
        highest = jnp.max(scores, axis=1, keepdims=True)
        exponent_terms = jnp.exp(scores - highest)
        weights = (exponent_terms / jnp.sum(exponent_terms, axis=1, keepdims=True)).astype(
            jnp.bfloat16
        )
        return jnp.dot(weights, value_head, preferred_element_type=jnp.float32)

    return lax.map(one_head, jnp.arange(query_rot.shape[1], dtype=jnp.int32))


def local(
    hidden,
    gain,
    w_query,
    key_matrix,
    value_matrix,
    passage_cache,
    passage_ids,
    placement,
    tile_index,
    tile_count,
):
    slot_rows = hidden.shape[0]
    gathered = lax.all_gather(hidden, "tp", axis=1, tiled=True)
    raw_values = gathered.astype(jnp.float32)
    inverse_rms = lax.rsqrt(jnp.mean(raw_values * raw_values, axis=1, keepdims=True) + 1e-05)
    normed_input = (raw_values * inverse_rms * gain.astype(jnp.float32)).astype(jnp.bfloat16)

    def add_rows(piece):
        return jnp.dot(normed_input, piece, preferred_element_type=jnp.float32)

    query_width = w_query.shape[1]
    kv_width = key_matrix.shape[1]
    query = add_rows(lax.all_gather(w_query, "store", axis=0, tiled=True))
    recomputed_key = add_rows(lax.all_gather(key_matrix, "store", axis=0, tiled=True))
    recomputed_value = add_rows(lax.all_gather(value_matrix, "store", axis=0, tiled=True))
    local_query_heads = query_width // HEAD_SIZE
    local_kv_heads = kv_width // HEAD_SIZE
    tiles = tile_index[0]
    used_count = tile_count[0]
    tile_size = slot_rows // tiles.shape[0]
    positions = (
        tiles[:, None] * tile_size + jnp.arange(tile_size, dtype=jnp.int32)[None, :]
    ).reshape(slot_rows)
    query_rot = rotate_pairs(
        query.reshape(slot_rows, local_query_heads, HEAD_SIZE), positions
    ).astype(jnp.bfloat16)
    rotated_key = rotate_pairs(
        recomputed_key.reshape(slot_rows, local_kv_heads, HEAD_SIZE), positions
    ).astype(jnp.bfloat16)
    value_fresh = recomputed_value.reshape(slot_rows, local_kv_heads, HEAD_SIZE).astype(
        jnp.bfloat16
    )
    fresh_rows = jnp.stack([rotated_key, value_fresh], axis=2).reshape(
        slot_rows, local_kv_heads * 2 * HEAD_SIZE
    )
    wanted = lax.all_gather(passage_ids, "store", axis=0, tiled=True)
    outgoing = passage_cache[wanted]
    incoming = lax.all_to_all(outgoing, "store", split_axis=0, concat_axis=0, tiled=True)
    groups = lax.axis_size("store")
    own_ids = passage_ids[0]
    turns = placement[own_ids]
    source = (jnp.arange(groups, dtype=jnp.int32)[None, :] - turns[:, None]) % groups
    ordered = incoming[source, jnp.arange(own_ids.shape[0], dtype=jnp.int32)[:, None]]
    context_output = ordered.reshape(-1, outgoing.shape[-1])
    context_rows = context_output.shape[0]
    for tile_slot in range(tiles.shape[0]):
        start = tiles[tile_slot] * tile_size
        current = lax.dynamic_slice_in_dim(context_output, start, tile_size, 0)
        update = jnp.where(
            tile_slot < used_count,
            fresh_rows[tile_slot * tile_size : (tile_slot + 1) * tile_size],
            current,
        )
        context_output = lax.dynamic_update_slice_in_dim(context_output, update, start, 0)
    blended_cache = context_output.reshape(context_rows, local_kv_heads, 2, HEAD_SIZE)
    allowed = jnp.arange(context_rows, dtype=jnp.int32)[None, :] <= positions[:, None]
    heads_out = attend_heads(
        query_rot,
        blended_cache[:, :, 0, :],
        blended_cache[:, :, 1, :],
        allowed,
        local_query_heads // local_kv_heads,
    )
    valid = jnp.arange(slot_rows, dtype=jnp.int32) // tile_size < used_count
    result = jnp.where(valid[:, None, None], jnp.transpose(heads_out, (1, 0, 2)), jnp.float32(0.0))
    return result.reshape(slot_rows, query_width).astype(jnp.bfloat16)


def solution(mesh):
    placed = (
        P("store", "tp"),
        P(),
        P("store", "tp"),
        P("store", "tp"),
        P("store", "tp"),
        P(None, "store", "tp"),
        P("store", None),
        P(),
        P("store", None),
        P("store"),
    )
    return jax.shard_map(
        local, mesh=mesh, in_specs=placed, out_specs=P("store", "tp"), check_vma=False
    )
```

profile of v0, /device:TPU:1, one launch (start us, length us, event | category | flops | bytes accessed | tf_op | source)
XLA Modules:
  0.0 404.5 jit_solution(11951558494705334625)
XLA Ops:
  9.3 36.3 %all-gather = s32[32,1,6]{2,1,0:T(1,128)S(1)} all-gather(s32[1,1,6]{2,1,0:T(1,128)} %bitcast.99), channel_id=1, replica_groups=mesh['store'=32,'tp'=8] {'store'}, dimensions={0}, use_global_device_ids=true | all-gather | bytes 792 | tf_op jit(solution)/shard_map/all_gather | solution.py:97
  45.8 2.7 gather_fusion
  48.5 5.6 %all-to-all-start = ((bf16[32,6,32,256]{3,2,1,0:T(8,128)(2,1)}), bf16[32,6,32,256]{3,2,1,0:T(8,128)(2,1)}, u32[]{:S(2)}, u32[]{:S(2)}) async-start(bf16[32,6,32,256]{3,2,1,0:T(8,128)(2,1)} %bitcast.89), calls=%async_computation | async-start | bytes 6291456 | tf_op jit(solution)/shard_map/all_to_all | solution.py:99
  60.8 60.6 %all-to-all-done = bf16[32,6,32,256]{3,2,1,0:T(8,128)(2,1)} async-done(((bf16[32,6,32,256]{3,2,1,0:T(8,128)(2,1)}), bf16[32,6,32,256]{3,2,1,0:T(8,128)(2,1)}, u32[]{:S(2)}, u32[]{:S(2)}) %all-to-all-start) | async-done | bytes 3145760 | tf_op jit(solution)/shard_map/all_to_all | solution.py:99
  121.4 5.3 %gather_fusion.2 = bf16[192,32,256]{2,1,0:T(8,128)(2,1)} fusion(bf16[32,6,32,256]{3,2,1,0:T(8,128)(2,1)} %all-to-all-done, s32[192]{0:T(256)S(1)} %reshape.357), kind=kCustom, calls=%fused_computation.2 | custom fusion | bytes 6292992 | tf_op jit(solution)/shard_map/gather | solution.py:104
  126.8 5.1 %fusion.15 = f32[512]{0:T(512)S(1)} fusion(bf16[512,8192]{1,0:T(8,128)(2,1)} %all-gather.6.cloned.1.call-done), kind=kLoop, calls=%fused_computation.19 | loop fusion | flops 12582400 | bytes 8390656 | tf_op jit(solution)/shard_map/reduce_sum | solution.py:66
  131.9 17.5 %all-gather.10.cloned.1.call-done = bf16[8192,128]{1,0:T(8,128)(2,1)} async-done(((bf16[256,128]{1,0:T(8,128)(2,1)}), bf16[8192,128]{1,0:T(8,128)(2,1)}) %all-gather.10.cloned.1.call-update) | async-done | bytes 2097168 | tf_op jit(solution)/shard_map/all_gather | solution.py:75
  149.4 6.5 %convolution_bitcast_fusion = f32[512,1,128]{0,2,1:T(8,128)S(1)} fusion(bf16[8192,128]{1,0:T(8,128)(2,1)} %all-gather.10.cloned.1.call-done, bf16[512,8192]{1,0:T(8,128)(2,1)} %all-gather.6.cloned.1.call-done, f32[8192]{0:T(1024)S(1)} %convert_element_type.45, f32[512]{0:T(512)S(1)} %add_rsqrt_fusion), kind=kOutput, calls=%fused_computation.22 | convolution fusion | flops 1090519040 | bytes 10782720 | tf_op jit(solution)/shard_map/dot_general | solution.py:70
  156.4 71.0 %all-gather.12.cloned.1.call-done = bf16[8192,128]{1,0:T(8,128)(2,1)} async-done(((bf16[256,128]{1,0:T(8,128)(2,1)}), bf16[8192,128]{1,0:T(8,128)(2,1)}) %all-gather.12.cloned.1.call-update) | async-done | bytes 2097168 | tf_op jit(solution)/shard_map/all_gather | solution.py:76
  227.4 7.0 %fusion.18 = bf16[512,1,1,128]{0,3,2,1:T(8,128)(2,1)S(1)} fusion(bf16[8192,128]{1,0:T(8,128)(2,1)} %all-gather.12.cloned.1.call-done, bf16[512,8192]{1,0:T(8,128)(2,1)} %all-gather.6.cloned.1.call-done, f32[8192]{0:T(1024)S(1)} %convert_element_type.45, f32[512]{0:T(512)S(1)} %add_rsqrt_fusion), kind=kOutput, calls=%fused_computation.24 | convolution fusion | flops 1090584576 | bytes 10651648 | tf_op jit(solution)/shard_map/dot_general | solution.py:70
  240.9 4.7 %copy.31 = bf16[6144,256]{0,1:T(8,128)(2,1)} copy(bf16[6144,256]{1,0:T(8,128)(2,1)} %select_dynamic-update-slice_fusion) | data formatting | bytes 6291456 | tf_op jit(solution)/shard_map/dynamic_update_slice | solution.py:115
  245.6 3.9 fusion.48
  249.5 2.6 copy.32
  254.7 74.4 %all-gather.8.cloned.1.call-done = bf16[8192,512]{1,0:T(8,128)(2,1)} async-done(((bf16[256,512]{1,0:T(8,128)(2,1)}), bf16[8192,512]{1,0:T(8,128)(2,1)}) %all-gather.8.cloned.1.call-update) | async-done | bytes 8388624 | tf_op jit(solution)/shard_map/all_gather | solution.py:74
  329.1 11.3 %fusion.45 = f32[512,512]{0,1:T(8,128)S(1)} fusion(bf16[8192,512]{1,0:T(8,128)(2,1)} %all-gather.8.cloned.1.call-done, bf16[512,8192]{1,0:T(8,128)(2,1)} %all-gather.6.cloned.1.call-done, f32[8192]{0:T(1024)S(1)} %convert_element_type.45, f32[512]{0:T(512)S(1)} %add_rsqrt_fusion), kind=kOutput, calls=%fused_computation.79 | convolution fusion | flops 4311744512 | bytes 17860608 | tf_op jit(solution)/shard_map/dot_general | solution.py:70
  347.1 48.9 %while.12 = (s32[]{:T(128)}, bf16[4,512,128]{2,1,0:T(8,128)(2,1)}, s32[4]{0:T(128)S(1)}, bf16[512,4,128]{2,0,1:T(8,128)(2,1)S(1)}, bf16[6144,1,128]{2,0,1:T(8,12...) while((s32[]{:T(128)}, bf16[4,512,128]{2,1,0:T(8,128)(2,1)}, ...), condition=%wide.region_4.5_spmd.clone.clone, body=%wide.region_1.4_spmd.clone.sunk.clone | while | flops 1638923264 | bytes 51785952 | solution.py:48
  349.7 3.8 fusion.65
  355.4 3.1 fusion.67
  361.9 3.8 fusion.65
  367.6 3.1 fusion.67
  374.1 3.8 fusion.65
  379.8 3.1 fusion.67
  386.3 3.8 fusion.65
  392.0 3.1 fusion.67
  (87 shorter events, 37.5 us)
Async XLA Ops:
  6.5 39.3 %copy-start = (bf16[128,32,256]{2,1,0:T(8,128)(2,1)S(1)}, bf16[128,32,256]{2,1,0:T(8,128)(2,1)}, u32[]{:S(2)}) copy-start(bf16[128,32,256]{2,1,0:T(8,128)(2,1)} %param.17) | copy-start | bytes 6291460
  6.5 50.9 %copy-start.7 = (s32[1,6]{1,0:T(1,128)S(1)}, s32[1,6]{1,0:T(1,128)}, u32[]{:S(2)}) copy-start(s32[1,6]{1,0:T(1,128)} %param.18) | copy-start | bytes 76
  6.5 47.6 %copy-start.6 = (s32[1,4]{1,0:T(1,128)S(1)}, s32[1,4]{1,0:T(1,128)}, u32[]{:S(2)}) copy-start(s32[1,4]{1,0:T(1,128)} %param.20) | copy-start | bytes 52
  6.5 50.9 %copy-start.5 = (bf16[8192]{0:T(1024)(128)(2,1)S(1)}, bf16[8192]{0:T(1024)(128)(2,1)}, u32[]{:S(2)}) copy-start(bf16[8192]{0:T(1024)(128)(2,1)} %param.13) | copy-start | bytes 49156
  6.5 50.9 %copy-start.1 = (s32[128]{0:T(128)S(1)}, s32[128]{0:T(128)}, u32[]{:S(2)}) copy-start(s32[128]{0:T(128)} %param.19) | copy-start | bytes 1540
  6.5 120.2 %all-gather.6.cloned.1.call-start = ((), (), s32[]{:S(2)}) async-start(), calls=%async_computation.1 | async-start | bytes 9437184 | tf_op jit(solution)/shard_map/all_gather | solution.py:64
  7.3 142.1 %all-gather.10.cloned.1.call-start = ((), (), s32[]{:S(2)}) async-start(), calls=%async_computation.3 | async-start | bytes 2162688 | tf_op jit(solution)/shard_map/all_gather | solution.py:75
  8.0 219.4 %all-gather.12.cloned.1.call-start = ((), (), s32[]{:S(2)}) async-start(), calls=%async_computation.4 | async-start | bytes 2162688 | tf_op jit(solution)/shard_map/all_gather | solution.py:76
  8.8 320.4 %all-gather.8.cloned.1.call-start = ((), (), s32[]{:S(2)}) async-start(), calls=%async_computation.2 | async-start | bytes 8650752 | tf_op jit(solution)/shard_map/all_gather | solution.py:74
  48.5 72.9 %all-to-all-start = ((bf16[32,6,32,256]{3,2,1,0:T(8,128)(2,1)}), bf16[32,6,32,256]{3,2,1,0:T(8,128)(2,1)}, u32[]{:S(2)}, u32[]{:S(2)}) async-start(bf16[32,6,32,256]{3,2,1,0:T(8,128)(2,1)} %bitcast.89), calls=%async_computation | async-start | bytes 6291456 | tf_op jit(solution)/shard_map/all_to_all | solution.py:99
  353.5 1.9 copy-start.2
  353.5 1.9 copy-start.3
  358.6 0.8 copy-start.4
  365.7 1.9 copy-start.2
  365.7 1.9 copy-start.3
  370.8 0.8 copy-start.4
  377.9 1.9 copy-start.2
  377.9 1.9 copy-start.3
  383.0 0.8 copy-start.4
  390.1 1.9 copy-start.2
  390.1 1.9 copy-start.3
  395.2 0.8 copy-start.4
Sparse Core Ops, SparseCore 0:
  9.2 56.4 all-gather.5
  68.3 81.0 all-gather.9
  152.0 75.4 all-gather.11
  229.9 99.1 all-gather.7
where the time goes:
time: 406 us; the launch traced here: 405 us
  waiting for transfers between devices  226 us (56%)
  matrix products  52.6 us (13%)
  blocking collectives  36.3 us (9%)
  local copies, waits for them, and re-layouts  34.1 us (8%)
  other arithmetic  25 us (6%)
  between operations  16.7 us (4%)
  loops' own time  7.96 us (2%)
  starting transfers between devices  5.75 us (1%)
    all_gather x1, waiting for transfers between devices, local(): query = add_rows(lax.all_gather(w_query, 'store', axis=0, tiled=True))  74.4 us
    all_gather x1, waiting for transfers between devices, local(): lax.all_gather(value_matrix, 'store', axis=0, tiled=True)  71 us
    all_to_all x1, waiting for transfers between devices, local(): lax.all_to_all(outgoing, 'store', split_axis=0, concat_axis=0, tiled=True)  60.6 us
    all_gather x1, blocking collectives, local(): wanted = lax.all_gather(passage_ids, 'store', axis=0, tiled=True)  36.3 us
    dot_general x3, matrix products, add_rows(): return jnp.dot(normed_input, piece, preferred_element_type=jnp.float32)  24.8 us
    all_gather x1, waiting for transfers between devices, local(): lax.all_gather(key_matrix, 'store', axis=0, tiled=True)  17.5 us
    dot_general x4, matrix products, one_head(): lax.dot_general(query_head, key_head, (((1,), (1,)), ((), ())), preferred...  15.3 us
    dot_general x4, matrix products, one_head(): return jnp.dot(weights, value_head, preferred_element_type=jnp.float32)  12.5 us
  transfers between devices with their start and end apart: 5, of which 4 were waited for; matrix products, arithmetic and copies ran while one was open for 13% of the time, Pallas kernels for 0%

commit v1 on v0

v1 whole, which is shorter than its diff:
```python
import math

import jax
import jax.numpy as jnp
from jax import lax
from jax.experimental import pallas as pl
from jax.experimental.pallas import tpu as pltpu
from jax.sharding import PartitionSpec as P

HEAD = 128
NY, NZ, NX = 4, 8, 4
N_STORE = NY * NZ
N_TP = 2 * NX
SLOTS = 512
TILE = 128
PASSAGES = 6
STRIPE = 32
CHUNK = 256
COLS = 768
FEATS = 1024
KEEP = 192
FULL = (0, CHUNK)
ZFIRST = (0, KEEP)
YFIRST = (KEEP, CHUNK)
MESH_ID = pl.DeviceIdType.MESH
SCORE = math.log2(math.e) / math.sqrt(HEAD)


def halves(rows):
    low, high = rows
    middle = (low + high) // 2
    return (low, middle), (middle, high)


def exchange_kernel(
    hidden, gain, wq, km, vm, cache, ids, tiles,
    q_out, kv_out, inbox,
    hbuf, wbuf, cbuf, outbox, idrow, idbuf, idmem, acc,
    load_sem, zr, zl, yu, yd, yu2, yd2, br, bl, hx, hs, idr, pr,
    zs, ys, ys2, bs, hxs, hss, ids_s, ps,
):
    st = lax.axis_index("store")
    tp = lax.axis_index("tp")
    y, z = st // NZ, st % NZ
    x, core = tp // 2, tp % 2
    sibling = x * 2 + (1 - core)

    def at_z(k):
        return y * NZ + (z + k + NZ) % NZ

    def at_y(k):
        return ((y + k + NY) % NY) * NZ + z

    def slot(dy, dz):
        return ((y + dy + NY) % NY) * NZ + (z + dz + NZ) % NZ

    def at_x(k):
        return ((x + k + NX) % NX) * 2 + core

    loads = [
        pltpu.make_async_copy(wq, wbuf.at[st, :, pl.ds(0, 512)], load_sem.at[0]),
        pltpu.make_async_copy(km, wbuf.at[st, :, pl.ds(512, 128)], load_sem.at[1]),
        pltpu.make_async_copy(vm, wbuf.at[st, :, pl.ds(640, 128)], load_sem.at[2]),
        pltpu.make_async_copy(hidden, hbuf.at[tp], load_sem.at[3]),
        pltpu.make_async_copy(cache, cbuf, load_sem.at[4]),
    ]
    for load in loads:
        load.start()
    idrow[...] = jnp.zeros_like(idrow)
    idrow[0:1, 0:PASSAGES] = ids[...]

    barrier = pltpu.get_barrier_semaphore()

    def greet(d, carry):
        pl.semaphore_signal(
            barrier, inc=1, device_id=((st + d) % N_STORE, tp), device_id_type=MESH_ID
        )
        return carry

    lax.fori_loop(1, N_STORE, greet, 0)
    for peer in (at_x(1), at_x(-1), sibling):
        pl.semaphore_signal(barrier, inc=1, device_id=(st, peer), device_id_type=MESH_ID)
    pl.semaphore_wait(barrier, N_STORE - 1 + 3)

    pending = []

    def send(ref, send_sem, recv_sem, store, peer, later=True):
        copy = pltpu.make_async_remote_copy(
            src_ref=ref, dst_ref=ref, send_sem=send_sem, recv_sem=recv_sem,
            device_id=(store, peer), device_id_type=MESH_ID,
        )
        copy.start()
        if later:
            pending.append(copy)
        return copy

    def arrived(ref, sem):
        pltpu.make_async_copy(ref, ref, sem).wait()

    def w_at(chunk, rows):
        return wbuf.at[chunk, pl.ds(rows[0], rows[1] - rows[0]), :]

    def id_copy(d):
        other = (st + d) % N_STORE
        return pltpu.make_async_remote_copy(
            src_ref=idrow, dst_ref=idbuf.at[st], send_sem=ids_s.at[d], recv_sem=idr.at[d],
            device_id=(other, tp), device_id_type=MESH_ID,
        )

    def id_start(d, carry):
        id_copy(d).start()
        return carry

    lax.fori_loop(1, N_STORE, id_start, 0)

    for load in loads:
        load.wait()
    own = w_at(st, FULL)
    send(own, zs.at[0], zr.at[1], at_z(1), tp)
    send(own, zs.at[1], zl.at[1], at_z(-1), tp)
    send(own, ys.at[0], yu.at[0], at_y(1), tp)
    send(own, ys.at[1], yd.at[0], at_y(-1), tp)
    h_sends = []
    h_own = hbuf.at[tp]
    h_sends.append(send(h_own, hxs.at[0], hx.at[0], st, at_x(1), False))
    h_sends.append(send(h_own, hxs.at[1], hx.at[1], st, at_x(-1), False))
    h_sends.append(send(h_own, hss.at[0], hs.at[0], st, sibling, False))

    idbuf[pl.ds(st, 1), :, :] = idrow[...].reshape(1, 1, 128)

    def id_wait(d, carry):
        other = (st - d + N_STORE) % N_STORE
        arrived(idbuf.at[other], idr.at[d])
        return carry

    lax.fori_loop(1, N_STORE, id_wait, 0)
    to_scalar = pltpu.make_async_copy(idbuf, idmem, load_sem.at[0])
    to_scalar.start()
    to_scalar.wait()

    def stripe_copy(d):
        other = (st + d) % N_STORE
        return pltpu.make_async_remote_copy(
            src_ref=outbox.at[other], dst_ref=inbox.at[st], send_sem=ps.at[d], recv_sem=pr.at[d],
            device_id=(other, tp), device_id_type=MESH_ID,
        )

    def fill(other):
        for j in range(PASSAGES):
            outbox[other, j * STRIPE : (j + 1) * STRIPE, :] = cbuf[idmem[other, 0, j]]

    def stripe_start(d, carry):
        fill((st + d) % N_STORE)
        stripe_copy(d).start()
        return carry

    lax.fori_loop(1, N_STORE, stripe_start, 0)
    fill(st)
    own_stripes = pltpu.make_async_copy(outbox.at[st], inbox.at[st], load_sem.at[1])
    own_stripes.start()

    def project(chunk):
        piece = chunk // 4
        column = pl.multiple_of((chunk % 4) * CHUNK, CHUNK)
        for m in range(2):
            rows = slice(m * 256, (m + 1) * 256)
            acc[rows, :] += jnp.dot(
                hbuf[piece, rows, pl.ds(column, CHUNK)], wbuf[chunk], preferred_element_type=jnp.float32
            )

    offsets = [0, -1, 1, -2, 2, -3, 3, 4]

    def forward_y(i):
        ref = w_at(slot(0, offsets[i]), ZFIRST)
        send(ref, ys.at[2 * i], yu.at[i], at_y(1), tp)
        send(ref, ys.at[2 * i + 1], yd.at[i], at_y(-1), tp)

    def ring(k):
        if k < 4:
            low, high = slot(0, -k), slot(0, k)
            arrived(w_at(low, FULL), zr.at[k])
            part = FULL if k < 3 else halves(FULL)[0]
            send(w_at(low, part), zs.at[2 * k], zr.at[k + 1], at_z(1), tp)
            arrived(w_at(high, FULL), zl.at[k])
            part = FULL if k < 3 else halves(FULL)[1]
            send(w_at(high, part), zs.at[2 * k + 1], zl.at[k + 1], at_z(-1), tp)
            forward_y(2 * k - 1)
            forward_y(2 * k)
        else:
            far = slot(0, 4)
            arrived(w_at(far, halves(FULL)[0]), zr.at[4])
            arrived(w_at(far, halves(FULL)[1]), zl.at[4])
            forward_y(7)

    def y_near(i):
        rows = FULL if i == 0 else ZFIRST
        top, bottom = halves(rows)
        below, above = slot(-1, offsets[i]), slot(1, offsets[i])
        arrived(w_at(below, rows), yu.at[i])
        send(w_at(below, top), ys2.at[2 * i], yu2.at[i], at_y(1), tp)
        arrived(w_at(above, rows), yd.at[i])
        send(w_at(above, bottom), ys2.at[2 * i + 1], yd2.at[i], at_y(-1), tp)

    def y_far(i):
        rows = FULL if i == 0 else ZFIRST
        top, bottom = halves(rows)
        far = slot(2, offsets[i])
        arrived(w_at(far, top), yu2.at[i])
        arrived(w_at(far, bottom), yd2.at[i])

    lines = [-1, 1, 2]

    def line_start(j):
        ref = w_at(slot(lines[j], 0), YFIRST)
        send(ref, bs.at[j, 0], br.at[j, 1], at_z(1), tp)
        send(ref, bs.at[j, 1], bl.at[j, 1], at_z(-1), tp)

    def line(j, k):
        if k < 4:
            low, high = slot(lines[j], -k), slot(lines[j], k)
            arrived(w_at(low, YFIRST), br.at[j, k])
            part = YFIRST if k < 3 else halves(YFIRST)[0]
            send(w_at(low, part), bs.at[j, 2 * k], br.at[j, k + 1], at_z(1), tp)
            arrived(w_at(high, YFIRST), bl.at[j, k])
            part = YFIRST if k < 3 else halves(YFIRST)[1]
            send(w_at(high, part), bs.at[j, 2 * k + 1], bl.at[j, k + 1], at_z(-1), tp)
        else:
            far = slot(lines[j], 4)
            arrived(w_at(far, halves(YFIRST)[0]), br.at[j, 4])
            arrived(w_at(far, halves(YFIRST)[1]), bl.at[j, 4])

    def h_near():
        low, high = at_x(-1), at_x(1)
        arrived(hbuf.at[low], hx.at[0])
        h_sends.append(send(hbuf.at[low, pl.ds(0, 256), :], hxs.at[2], hx.at[2], st, at_x(1), False))
        h_sends.append(send(hbuf.at[low], hss.at[1], hs.at[1], st, sibling, False))
        arrived(hbuf.at[high], hx.at[1])
        h_sends.append(send(hbuf.at[high, pl.ds(256, 256), :], hxs.at[3], hx.at[3], st, at_x(-1), False))
        h_sends.append(send(hbuf.at[high], hss.at[2], hs.at[2], st, sibling, False))

    def h_far():
        far = at_x(2)
        arrived(hbuf.at[far, pl.ds(0, 256), :], hx.at[2])
        arrived(hbuf.at[far, pl.ds(256, 256), :], hx.at[3])
        h_sends.append(send(hbuf.at[far], hss.at[3], hs.at[3], st, sibling, False))

    def h_norm():
        for i, k in enumerate((0, -1, 1, 2)):
            piece = ((x + k + NX) % NX) * 2 + (1 - core)
            arrived(hbuf.at[piece], hs.at[i])
        for copy in h_sends:
            copy.wait_send()

        def block(b, carry):
            rows = pl.ds(pl.multiple_of(b * 32, 32), 32)
            total = jnp.zeros((32, 1), jnp.float32)
            for p in range(N_TP):
                raw = hbuf[p, rows, :].astype(jnp.float32)
                total += jnp.sum(raw * raw, axis=1, keepdims=True)
            scale = lax.rsqrt(total / (N_TP * FEATS) + 1e-05)
            for p in range(N_TP):
                raw = hbuf[p, rows, :].astype(jnp.float32)
                row_gain = gain[:, p * FEATS : (p + 1) * FEATS].astype(jnp.float32)
                hbuf[p, rows, :] = (raw * scale * row_gain).astype(jnp.bfloat16)
            return carry

        lax.fori_loop(0, SLOTS // 32, block, 0)

    acc[...] = jnp.zeros_like(acc)

    ring(1)
    y_near(0)
    line_start(0)
    line_start(1)
    ring(2)
    h_near()
    y_far(0)
    line_start(2)
    y_near(1)
    y_near(2)
    line(0, 1)
    line(1, 1)
    ring(3)
    h_far()
    y_near(3)
    y_near(4)
    line(2, 1)
    line(0, 2)
    line(1, 2)
    ring(4)
    h_norm()

    def project_row(dy):
        def step(i, carry):
            project(((y + dy + NY) % NY) * NZ + i)
            return carry

        lax.fori_loop(0, NZ, step, 0)

    y_near(5)
    y_near(6)
    line(2, 2)
    line(0, 3)
    line(1, 3)
    y_near(7)
    line(2, 3)
    project_row(0)
    line(0, 4)
    line(1, 4)
    project_row(-1)
    project_row(1)
    line(2, 4)
    for i in range(1, 8):
        y_far(i)
    project_row(2)

    lane = lax.broadcasted_iota(jnp.int32, (TILE, HEAD), 1)
    frequency = jnp.exp((lane % (HEAD // 2)).astype(jnp.float32) * (-math.log(500000.0) * 2.0 / HEAD))
    for s in range(SLOTS // TILE):
        rows = slice(s * TILE, (s + 1) * TILE)
        position = lax.broadcasted_iota(jnp.int32, (TILE, HEAD), 0) + tiles[0, s] * TILE
        angle = position.astype(jnp.float32) * frequency
        cosine = jnp.cos(angle)
        sine = jnp.where(lane < HEAD // 2, -jnp.sin(angle), jnp.sin(angle))
        for h in range(5):
            vec = acc[rows, h * HEAD : (h + 1) * HEAD]
            turned = vec * cosine + pltpu.roll(vec, HEAD // 2, 1) * sine
            if h < 4:
                q_out[h, rows, :] = turned.astype(jnp.bfloat16)
            else:
                kv_out[rows, 0:HEAD] = turned.astype(jnp.bfloat16)
        kv_out[rows, HEAD : 2 * HEAD] = acc[rows, 5 * HEAD : 6 * HEAD].astype(jnp.bfloat16)

    def stripe_wait(d, carry):
        other = (st - d + N_STORE) % N_STORE
        arrived(inbox.at[other], pr.at[d])
        stripe_copy(d).wait_send()
        id_copy(d).wait_send()
        return carry

    lax.fori_loop(1, N_STORE, stripe_wait, 0)
    own_stripes.wait()
    for copy in pending:
        copy.wait_send()


def exchange(hidden, gain, wq, km, vm, cache, ids, tiles):
    any_space = pl.BlockSpec(memory_space=pl.ANY)
    vmem = pl.BlockSpec(memory_space=pltpu.VMEM)
    smem = pl.BlockSpec(memory_space=pltpu.SMEM)
    dma = pltpu.SemaphoreType.DMA
    return pl.pallas_call(
        exchange_kernel,
        out_shape=[
            jax.ShapeDtypeStruct((4, SLOTS, HEAD), jnp.bfloat16),
            jax.ShapeDtypeStruct((SLOTS, 2 * HEAD), jnp.bfloat16),
            jax.ShapeDtypeStruct((N_STORE, PASSAGES * STRIPE, 2 * HEAD), jnp.bfloat16),
        ],
        in_specs=[any_space, vmem, any_space, any_space, any_space, any_space, vmem, smem],
        out_specs=[vmem, vmem, any_space],
        scratch_shapes=[
            pltpu.VMEM((N_TP, SLOTS, FEATS), jnp.bfloat16),
            pltpu.VMEM((N_STORE, CHUNK, COLS), jnp.bfloat16),
            pltpu.VMEM((128, STRIPE, 2 * HEAD), jnp.bfloat16),
            pltpu.VMEM((N_STORE, PASSAGES * STRIPE, 2 * HEAD), jnp.bfloat16),
            pltpu.VMEM((1, 128), jnp.int32),
            pltpu.VMEM((N_STORE, 1, 128), jnp.int32),
            pltpu.SMEM((N_STORE, 1, 128), jnp.int32),
            pltpu.VMEM((SLOTS, COLS), jnp.float32),
            dma((5,)),
            dma((5,)), dma((5,)), dma((8,)), dma((8,)), dma((8,)), dma((8,)),
            dma((3, 5)), dma((3, 5)), dma((4,)), dma((4,)), dma((32,)), dma((32,)),
            dma((8,)), dma((16,)), dma((16,)), dma((3, 8)), dma((4,)), dma((4,)), dma((32,)), dma((32,)),
        ],
        compiler_params=pltpu.CompilerParams(
            collective_id=0, has_side_effects=True, vmem_limit_bytes=48 * 2**20
        ),
    )(hidden, gain, wq, km, vm, cache, ids, tiles)


KEYS = 512


def attend_kernel(ids, placement, tiles, count, q, kv, inbox, out, context, scores, highest, total, values):
    for j in range(PASSAGES):
        turn = placement[ids[0, j]]

        def order(i, carry):
            source = (i - turn + N_STORE) % N_STORE
            rows = pl.ds(pl.multiple_of(j * 1024 + i * STRIPE, STRIPE), STRIPE)
            context[rows, :] = inbox[source, j * STRIPE : (j + 1) * STRIPE, :]
            return carry

        lax.fori_loop(0, N_STORE, order, 0)
    for s in range(SLOTS // TILE):
        @pl.when(s < count[0])
        def _():
            rows = pl.ds(pl.multiple_of(tiles[0, s] * TILE, TILE), TILE)
            context[rows, :] = kv[s * TILE : (s + 1) * TILE, :]

    def one_slot(s, carry):
        slot_rows = pl.ds(pl.multiple_of(s * TILE, TILE), TILE)

        @pl.when(s >= count[0])
        def _():
            out[slot_rows, :] = jnp.zeros((TILE, 4 * HEAD), jnp.bfloat16)

        @pl.when(s < count[0])
        def _():
            tile = tiles[0, s]
            last = tile // (KEYS // TILE)
            query = q[:, slot_rows, :].reshape(4 * TILE, HEAD)

            def block_scores(b):
                keys = context[pl.ds(pl.multiple_of(b * KEYS, KEYS), KEYS), 0:HEAD]
                return lax.dot_general(
                    query, keys, (((1,), (1,)), ((), ())), preferred_element_type=jnp.float32
                )

            def widest(block):
                top = block[:, 0:HEAD]
                for n in range(1, KEYS // HEAD):
                    top = jnp.maximum(top, block[:, n * HEAD : (n + 1) * HEAD])
                return top

            block = block_scores(last)
            row = lax.broadcasted_iota(jnp.int32, (4 * TILE, KEYS), 0) % TILE + tile * TILE
            column = lax.broadcasted_iota(jnp.int32, (4 * TILE, KEYS), 1) + last * KEYS
            block = jnp.where(column <= row, block, -jnp.inf)
            scores[last] = block
            highest[...] = widest(block)

            def first_pass(b, carry):
                block = block_scores(b)
                scores[b] = block
                highest[...] = jnp.maximum(highest[...], widest(block))
                return carry

            lax.fori_loop(0, last, first_pass, 0)
            shift = jnp.max(highest[...], axis=1, keepdims=True) * SCORE
            total[...] = jnp.zeros_like(total)
            values[...] = jnp.zeros_like(values)

            def second_pass(b, carry):
                terms = jnp.exp2(scores[b] * SCORE - shift)
                part = terms[:, 0:HEAD]
                for n in range(1, KEYS // HEAD):
                    part = part + terms[:, n * HEAD : (n + 1) * HEAD]
                total[...] += part
                rows = pl.ds(pl.multiple_of(b * KEYS, KEYS), KEYS)
                values[...] += jnp.dot(
                    terms.astype(jnp.bfloat16), context[rows, HEAD : 2 * HEAD],
                    preferred_element_type=jnp.float32,
                )
                return carry

            lax.fori_loop(0, last + 1, second_pass, 0)
            result = values[...] / jnp.sum(total[...], axis=1, keepdims=True)
            for h in range(4):
                out[slot_rows, h * HEAD : (h + 1) * HEAD] = result[h * TILE : (h + 1) * TILE, :].astype(
                    jnp.bfloat16
                )

        return carry

    lax.fori_loop(0, SLOTS // TILE, one_slot, 0)


def attend(ids, placement, tiles, count, q, kv, inbox):
    vmem = pl.BlockSpec(memory_space=pltpu.VMEM)
    smem = pl.BlockSpec(memory_space=pltpu.SMEM)
    return pl.pallas_call(
        attend_kernel,
        out_shape=jax.ShapeDtypeStruct((SLOTS, 4 * HEAD), jnp.bfloat16),
        in_specs=[smem, smem, smem, smem, vmem, vmem, vmem],
        out_specs=vmem,
        scratch_shapes=[
            pltpu.VMEM((PASSAGES * 1024, 2 * HEAD), jnp.bfloat16),
            pltpu.VMEM((PASSAGES * 1024 // KEYS, 4 * TILE, KEYS), jnp.float32),
            pltpu.VMEM((4 * TILE, HEAD), jnp.float32),
            pltpu.VMEM((4 * TILE, HEAD), jnp.float32),
            pltpu.VMEM((4 * TILE, HEAD), jnp.float32),
        ],
        compiler_params=pltpu.CompilerParams(vmem_limit_bytes=48 * 2**20),
    )(ids, placement, tiles, count, q, kv, inbox)


def local(hidden, gain, w_query, key_matrix, value_matrix, passage_cache, passage_ids, placement, tile_index, tile_count):
    q, kv, inbox = exchange(
        hidden, gain.reshape(1, -1), w_query, key_matrix, value_matrix, passage_cache, passage_ids, tile_index
    )
    return attend(passage_ids, placement, tile_index, tile_count, q, kv, inbox)


def solution(mesh):
    placed = (
        P("store", "tp"), P(), P("store", "tp"), P("store", "tp"), P("store", "tp"),
        P(None, "store", "tp"), P("store", None), P(), P("store", None), P("store"),
    )
    return jax.shard_map(local, mesh=mesh, in_specs=placed, out_specs=P("store", "tp"), check_vma=False)
```

time: 406 us -> 189 us (0.47)
  the two profiles are of different devices: /device:TPU:1 before, /device:TPU:80 now
where the time goes in v1:
time: 189 us
  Pallas kernels  179 us (95%)
  local copies, waits for them, and re-layouts  9.37 us (5%)
    pallas_call x1, Pallas kernels, exchange(): pl.pallas_call(exchange_kernel, out_shape=[jax.ShapeDtypeStruct((4, SLOTS...  159 us
    pallas_call x1, Pallas kernels, attend(): pl.pallas_call(attend_kernel, out_shape=jax.ShapeDtypeStruct((SLOTS, 4 *...  19.9 us
    unnamed x20, local copies, waits for them, and re-layouts  8.64 us

profile of v1, /device:TPU:80, one launch (start us, length us, event | category | flops | bytes accessed | tf_op | source)
XLA Modules:
  0.0 188.9 jit_solution(3336938027353353316)
XLA Ops:
  0.0 0.0 copy-start.7
  0.0 0.0 copy-start.9
  0.7 0.7 reshape.3.gain
  1.4 0.0 copy-start.1
  1.4 1.6 copy-done.1
  3.0 0.0 copy-start.2
  3.0 1.2 copy-done.2
  4.2 0.0 copy-start.3
  4.2 0.9 copy-done.3
  5.2 0.0 copy-start.4
  5.2 0.8 copy-done.4
  6.0 0.0 copy-start.5
  6.0 0.8 copy-done.5
  6.9 0.0 copy-start.6
  6.9 0.7 copy-done.6
  7.5 0.0 copy-start.8
  7.5 0.7 copy-done.8
  8.2 158.8 %shard_map.100 = (bf16[4,512,128]{2,1,0:T(8,128)(2,1)S(1)}, bf16[512,256]{1,0:T(8,128)(2,1)S(1)}, bf16[32,192,256]{2,1,0:T(8,128)(2,1)}) custom-call(bf16[512,1024]{1,0:T(8,128)(2,1)S(1)} %copy-done.2, bf16[1,8192]{1,0:T(2,128)(2,1)S(1)} %reshape.3.gain, bf16[256,512]{1,0:T(8,128)(2,1)S(1)} %copy-done.3, bf16[256,128]{1,0:T(8,128)(2,1)S(1)} %copy-done.4, ...), custom_call_target="tpu_custom_call" | custom-call | tf_op jit(solution)/shard_map/pallas_call | solution.py:352
  167.0 0.0 copy-done.7
  167.0 0.0 copy-done.9
  167.0 0.0 copy-start
  167.0 1.9 copy-done
  168.9 19.9 %shard_map.101 = bf16[512,512]{1,0:T(8,128)(2,1)} custom-call(s32[1,6]{1,0:T(1,128)S(1)} %copy-done.7, s32[128]{0:T(128)S(1)} %copy-done.9, s32[1,4]{1,0:T(1,128)S(1)} %copy-done.8, s32[1]{0:T(128)S(6)} %copy.11.count, bf16[4,512,128]{2,1,0:T(8,128)(2,1)S(1)} %get-tuple-element.8.q, bf16[512,256]{1,0:T(8,128)(2,1)S(1)} %get-tuple-element.9.kv, ...), custom_call_target="tpu_custom_call" | custom-call | tf_op jit(solution)/shard_map/pallas_call | solution.py:472
Async XLA Ops:
  0.0 167.0 %copy-start.7 = (s32[1,6]{1,0:T(1,128)S(1)}, s32[1,6]{1,0:T(1,128)}, u32[]{:S(2)}) copy-start(s32[1,6]{1,0:T(1,128)} %ids.3) | copy-start | bytes 76
  0.0 167.0 %copy-start.9 = (s32[128]{0:T(128)S(1)}, s32[128]{0:T(128)}, u32[]{:S(2)}) copy-start(s32[128]{0:T(128)} %placement.1) | copy-start | bytes 1540
  1.4 1.6 copy-start.1
  3.0 1.2 copy-start.2
  4.2 0.9 copy-start.3
  5.2 0.8 copy-start.4
  6.0 0.8 copy-start.5
  6.9 0.7 copy-start.6
  7.5 0.7 copy-start.8
  167.0 1.9 %copy-start = (bf16[32,192,256]{2,1,0:T(8,128)(2,1)S(1)}, bf16[32,192,256]{2,1,0:T(8,128)(2,1)}, u32[]{:S(2)}) copy-start(bf16[32,192,256]{2,1,0:T(8,128)(2,1)} %get-tuple-element.10.inbox) | copy-start | bytes 9437188

commit v2 on v1

--- a/solution.py
+++ b/solution.py
@@ -154,10 +154,19 @@
         stripe_copy(d).start()
         return carry
 
-    lax.fori_loop(1, N_STORE, stripe_start, 0)
     fill(st)
     own_stripes = pltpu.make_async_copy(outbox.at[st], inbox.at[st], load_sem.at[1])
     own_stripes.start()
+
+    progress = [0, 1]
+
+    def trickle():
+        progress[0] += 1
+        if progress[0] > 4:
+            stop = min(N_STORE, progress[1] + 2)
+            for d in range(progress[1], stop):
+                stripe_start(d, 0)
+            progress[1] = stop
 
     def project(chunk):
         piece = chunk // 4
@@ -268,26 +277,39 @@
 
     acc[...] = jnp.zeros_like(acc)
 
+    trickle()
     ring(1)
+    trickle()
     y_near(0)
+    trickle()
     line_start(0)
     line_start(1)
     ring(2)
+    trickle()
     h_near()
+    trickle()
     y_far(0)
     line_start(2)
     y_near(1)
+    trickle()
     y_near(2)
+    trickle()
     line(0, 1)
     line(1, 1)
+    trickle()
     ring(3)
+    trickle()
     h_far()
     y_near(3)
+    trickle()
     y_near(4)
+    trickle()
     line(2, 1)
     line(0, 2)
+    trickle()
     line(1, 2)
     ring(4)
+    trickle()
     h_norm()
 
     def project_row(dy):
@@ -298,12 +320,19 @@
         lax.fori_loop(0, NZ, step, 0)
 
     y_near(5)
+    trickle()
     y_near(6)
+    trickle()
     line(2, 2)
+    trickle()
     line(0, 3)
+    trickle()
     line(1, 3)
     y_near(7)
+    trickle()
     line(2, 3)
+    for d in range(progress[1], N_STORE):
+        stripe_start(d, 0)
     project_row(0)
     line(0, 4)
     line(1, 4)
@@ -373,7 +402,7 @@
             dma((8,)), dma((16,)), dma((16,)), dma((3, 8)), dma((4,)), dma((4,)), dma((32,)), dma((32,)),
         ],
         compiler_params=pltpu.CompilerParams(
-            collective_id=0, has_side_effects=True, vmem_limit_bytes=48 * 2**20
+            collective_id=0, has_side_effects=True, vmem_limit_bytes=62 * 2**20
         ),
     )(hidden, gain, wq, km, vm, cache, ids, tiles)
 
@@ -481,7 +510,7 @@
             pltpu.VMEM((4 * TILE, HEAD), jnp.float32),
             pltpu.VMEM((4 * TILE, HEAD), jnp.float32),
         ],
-        compiler_params=pltpu.CompilerParams(vmem_limit_bytes=48 * 2**20),
+        compiler_params=pltpu.CompilerParams(vmem_limit_bytes=62 * 2**20),
     )(ids, placement, tiles, count, q, kv, inbox)
 
 

time: 189 us -> 168 us (0.89)
  the two profiles are of different devices: /device:TPU:80 before, /device:TPU:1 now
where the time goes in v2:
time: 168 us; the launch traced here: 167 us
  Pallas kernels  165 us (98%)
    pallas_call x1, Pallas kernels, exchange(): pl.pallas_call(exchange_kernel, out_shape=[jax.ShapeDtypeStruct((4, SLOTS...  140 us
    pallas_call x1, Pallas kernels, attend(): pl.pallas_call(attend_kernel, out_shape=jax.ShapeDtypeStruct((SLOTS, 4 *...  25.1 us

profile of v2, /device:TPU:1, one launch (start us, length us, event | category | flops | bytes accessed | tf_op | source)
XLA Modules:
  0.0 166.7 jit_solution(434013121927029557)
XLA Ops:
  0.7 1.4 reshape.3.gain
  2.0 139.6 %shard_map.100 = (bf16[4,512,128]{2,1,0:T(8,128)(2,1)}, bf16[512,256]{1,0:T(8,128)(2,1)}, bf16[32,192,256]{2,1,0:T(8,128)(2,1)}) custom-call(bf16[512,1024]{1,0:T(8,128)(2,1)} %hidden.1, bf16[1,8192]{1,0:T(2,128)(2,1)} %reshape.3.gain, bf16[256,512]{1,0:T(8,128)(2,1)} %wq.1, bf16[256,128]{1,0:T(8,128)(2,1)} %km.1, bf16[256,128]{1,0:T(8,128)(2,1)} %vm.1, ...), custom_call_target="tpu_custom_call" | custom-call | tf_op jit(solution)/shard_map/pallas_call | solution.py:381
  141.6 25.1 %shard_map.101 = bf16[512,512]{1,0:T(8,128)(2,1)} custom-call(s32[1,6]{1,0:T(1,128)} %ids.3, s32[128]{0:T(128)} %placement.1, s32[1,4]{1,0:T(1,128)} %tiles.3, s32[1]{0:T(128)S(6)} %copy.11.count, bf16[4,512,128]{2,1,0:T(8,128)(2,1)} %get-tuple-element.8.q, bf16[512,256]{1,0:T(8,128)(2,1)} %get-tuple-element.9.kv, bf16[32,192,256]{2,1,0:T(8,128)(2,1)} %get-tuple-element.10.inbox), custom_call_target="tpu_custom_call" | custom-call | tf_op jit(solution)/shard_map/pallas_call | solution.py:501

commit v3 on v2

--- a/solution.py
+++ b/solution.py
@@ -35,7 +35,7 @@
 def exchange_kernel(
     hidden, gain, wq, km, vm, cache, ids, tiles,
     q_out, kv_out, inbox,
-    hbuf, wbuf, cbuf, outbox, idrow, idbuf, idmem, acc,
+    hbuf, wbuf, cbuf, outbox, idrow, idbuf, idmem, acc, turn,
     load_sem, zr, zl, yu, yd, yu2, yd2, br, bl, hx, hs, idr, pr,
     zs, ys, ys2, bs, hxs, hss, ids_s, ps,
 ):
@@ -269,7 +269,7 @@
             scale = lax.rsqrt(total / (N_TP * FEATS) + 1e-05)
             for p in range(N_TP):
                 raw = hbuf[p, rows, :].astype(jnp.float32)
-                row_gain = gain[:, p * FEATS : (p + 1) * FEATS].astype(jnp.float32)
+                row_gain = gain[p * FEATS : (p + 1) * FEATS].astype(jnp.float32).reshape(1, FEATS)
                 hbuf[p, rows, :] = (raw * scale * row_gain).astype(jnp.bfloat16)
             return carry
 
@@ -311,6 +311,14 @@
     ring(4)
     trickle()
     h_norm()
+
+    lane = lax.broadcasted_iota(jnp.int32, (TILE, HEAD), 1)
+    frequency = jnp.exp((lane % (HEAD // 2)).astype(jnp.float32) * (-math.log(500000.0) * 2.0 / HEAD))
+    for s in range(SLOTS // TILE):
+        position = lax.broadcasted_iota(jnp.int32, (TILE, HEAD), 0) + tiles[0, s] * TILE
+        angle = position.astype(jnp.float32) * frequency
+        turn[0, s] = jnp.cos(angle)
+        turn[1, s] = jnp.where(lane < HEAD // 2, -jnp.sin(angle), jnp.sin(angle))
 
     def project_row(dy):
         def step(i, carry):
@@ -339,21 +347,24 @@
     project_row(-1)
     project_row(1)
     line(2, 4)
-    for i in range(1, 8):
-        y_far(i)
-    project_row(2)
-
-    lane = lax.broadcasted_iota(jnp.int32, (TILE, HEAD), 1)
-    frequency = jnp.exp((lane % (HEAD // 2)).astype(jnp.float32) * (-math.log(500000.0) * 2.0 / HEAD))
+    project(slot(2, 0))
+
+    def far_step(i, carry):
+        offset = ((i + 1) // 2) * (1 - 2 * (i % 2))
+        chunk = ((y + 2) % NY) * NZ + (z + offset + NZ) % NZ
+        top_rows, bottom_rows = halves(ZFIRST)
+        arrived(w_at(chunk, top_rows), yu2.at[i])
+        arrived(w_at(chunk, bottom_rows), yd2.at[i])
+        project(chunk)
+        return carry
+
+    lax.fori_loop(1, NZ, far_step, 0)
+
     for s in range(SLOTS // TILE):
         rows = slice(s * TILE, (s + 1) * TILE)
-        position = lax.broadcasted_iota(jnp.int32, (TILE, HEAD), 0) + tiles[0, s] * TILE
-        angle = position.astype(jnp.float32) * frequency
-        cosine = jnp.cos(angle)
-        sine = jnp.where(lane < HEAD // 2, -jnp.sin(angle), jnp.sin(angle))
         for h in range(5):
             vec = acc[rows, h * HEAD : (h + 1) * HEAD]
-            turned = vec * cosine + pltpu.roll(vec, HEAD // 2, 1) * sine
+            turned = vec * turn[0, s] + pltpu.roll(vec, HEAD // 2, 1) * turn[1, s]
             if h < 4:
                 q_out[h, rows, :] = turned.astype(jnp.bfloat16)
             else:
@@ -396,6 +407,7 @@
             pltpu.VMEM((N_STORE, 1, 128), jnp.int32),
             pltpu.SMEM((N_STORE, 1, 128), jnp.int32),
             pltpu.VMEM((SLOTS, COLS), jnp.float32),
+            pltpu.VMEM((2, 4, TILE, HEAD), jnp.float32),
             dma((5,)),
             dma((5,)), dma((5,)), dma((8,)), dma((8,)), dma((8,)), dma((8,)),
             dma((3, 5)), dma((3, 5)), dma((4,)), dma((4,)), dma((32,)), dma((32,)),
@@ -407,25 +419,31 @@
     )(hidden, gain, wq, km, vm, cache, ids, tiles)
 
 
-KEYS = 512
-
-
-def attend_kernel(ids, placement, tiles, count, q, kv, inbox, out, context, scores, highest, total, values):
-    for j in range(PASSAGES):
-        turn = placement[ids[0, j]]
-
-        def order(i, carry):
-            source = (i - turn + N_STORE) % N_STORE
-            rows = pl.ds(pl.multiple_of(j * 1024 + i * STRIPE, STRIPE), STRIPE)
-            context[rows, :] = inbox[source, j * STRIPE : (j + 1) * STRIPE, :]
-            return carry
-
-        lax.fori_loop(0, N_STORE, order, 0)
+KEYS = 1024
+STR = KEYS // STRIPE
+PER = 1024 // KEYS
+
+
+def attend_kernel(ids, placement, tiles, count, q, kv, inbox, out, stripes, scores, highest, total, values, sem):
+    load = pltpu.make_async_copy(inbox, stripes, sem)
+    load.start()
+    load.wait()
+
+    def block_of(b, lanes):
+        j = b // PER
+        first = b % PER * STR + N_STORE - placement[ids[0, j]]
+        rows = pl.ds(pl.multiple_of(j * STRIPE, STRIPE), STRIPE)
+        return jnp.concatenate([stripes[(first + k) % N_STORE, rows, lanes] for k in range(STR)], axis=0)
+
     for s in range(SLOTS // TILE):
         @pl.when(s < count[0])
         def _():
-            rows = pl.ds(pl.multiple_of(tiles[0, s] * TILE, TILE), TILE)
-            context[rows, :] = kv[s * TILE : (s + 1) * TILE, :]
+            j = tiles[0, s] // 8
+            first = tiles[0, s] % 8 * 4 + N_STORE - placement[ids[0, j]]
+            rows = pl.ds(pl.multiple_of(j * STRIPE, STRIPE), STRIPE)
+            for k in range(4):
+                part = s * TILE + k * STRIPE
+                stripes[(first + k) % N_STORE, rows, :] = kv[part : part + STRIPE, :]
 
     def one_slot(s, carry):
         slot_rows = pl.ds(pl.multiple_of(s * TILE, TILE), TILE)
@@ -441,9 +459,8 @@
             query = q[:, slot_rows, :].reshape(4 * TILE, HEAD)
 
             def block_scores(b):
-                keys = context[pl.ds(pl.multiple_of(b * KEYS, KEYS), KEYS), 0:HEAD]
                 return lax.dot_general(
-                    query, keys, (((1,), (1,)), ((), ())), preferred_element_type=jnp.float32
+                    query, block_of(b, slice(0, HEAD)), (((1,), (1,)), ((), ())), preferred_element_type=jnp.float32
                 )
 
             def widest(block):
@@ -459,41 +476,45 @@
             scores[last] = block
             highest[...] = widest(block)
 
-            def first_pass(b, carry):
+            def first_step(b):
                 block = block_scores(b)
                 scores[b] = block
                 highest[...] = jnp.maximum(highest[...], widest(block))
-                return carry
-
-            lax.fori_loop(0, last, first_pass, 0)
-            shift = jnp.max(highest[...], axis=1, keepdims=True) * SCORE
-            total[...] = jnp.zeros_like(total)
-            values[...] = jnp.zeros_like(values)
-
-            def second_pass(b, carry):
+
+            def second_step(b):
                 terms = jnp.exp2(scores[b] * SCORE - shift)
                 part = terms[:, 0:HEAD]
                 for n in range(1, KEYS // HEAD):
                     part = part + terms[:, n * HEAD : (n + 1) * HEAD]
                 total[...] += part
-                rows = pl.ds(pl.multiple_of(b * KEYS, KEYS), KEYS)
                 values[...] += jnp.dot(
-                    terms.astype(jnp.bfloat16), context[rows, HEAD : 2 * HEAD],
-                    preferred_element_type=jnp.float32,
+                    terms.astype(jnp.bfloat16), block_of(b, slice(HEAD, 2 * HEAD)), preferred_element_type=jnp.float32
                 )
-                return carry
-
-            lax.fori_loop(0, last + 1, second_pass, 0)
+
+            def over(step, n):
+                def pair(i, carry):
+                    step(2 * i)
+                    step(2 * i + 1)
+                    return carry
+
+                lax.fori_loop(0, n // 2, pair, 0)
+
+                @pl.when(n % 2 == 1)
+                def _():
+                    step(n - 1)
+
+            over(first_step, last)
+            shift = jnp.max(highest[...], axis=1, keepdims=True) * SCORE
+            total[...] = jnp.zeros_like(total)
+            values[...] = jnp.zeros_like(values)
+            over(second_step, last + 1)
             result = values[...] / jnp.sum(total[...], axis=1, keepdims=True)
             for h in range(4):
-                out[slot_rows, h * HEAD : (h + 1) * HEAD] = result[h * TILE : (h + 1) * TILE, :].astype(
-                    jnp.bfloat16
-                )
+                out[slot_rows, h * HEAD : (h + 1) * HEAD] = result[h * TILE : (h + 1) * TILE, :].astype(jnp.bfloat16)
 
         return carry
 
     lax.fori_loop(0, SLOTS // TILE, one_slot, 0)
-
 
 def attend(ids, placement, tiles, count, q, kv, inbox):
     vmem = pl.BlockSpec(memory_space=pltpu.VMEM)
@@ -501,14 +522,15 @@
     return pl.pallas_call(
         attend_kernel,
         out_shape=jax.ShapeDtypeStruct((SLOTS, 4 * HEAD), jnp.bfloat16),
-        in_specs=[smem, smem, smem, smem, vmem, vmem, vmem],
+        in_specs=[smem, smem, smem, smem, vmem, vmem, pl.BlockSpec(memory_space=pl.ANY)],
         out_specs=vmem,
         scratch_shapes=[
-            pltpu.VMEM((PASSAGES * 1024, 2 * HEAD), jnp.bfloat16),
+            pltpu.VMEM((N_STORE, PASSAGES * STRIPE, 2 * HEAD), jnp.bfloat16),
             pltpu.VMEM((PASSAGES * 1024 // KEYS, 4 * TILE, KEYS), jnp.float32),
             pltpu.VMEM((4 * TILE, HEAD), jnp.float32),
             pltpu.VMEM((4 * TILE, HEAD), jnp.float32),
             pltpu.VMEM((4 * TILE, HEAD), jnp.float32),
+            pltpu.SemaphoreType.DMA,
         ],
         compiler_params=pltpu.CompilerParams(vmem_limit_bytes=62 * 2**20),
     )(ids, placement, tiles, count, q, kv, inbox)
@@ -516,7 +538,7 @@
 
 def local(hidden, gain, w_query, key_matrix, value_matrix, passage_cache, passage_ids, placement, tile_index, tile_count):
     q, kv, inbox = exchange(
-        hidden, gain.reshape(1, -1), w_query, key_matrix, value_matrix, passage_cache, passage_ids, tile_index
+        hidden, gain, w_query, key_matrix, value_matrix, passage_cache, passage_ids, tile_index
     )
     return attend(passage_ids, placement, tile_index, tile_count, q, kv, inbox)
 

time: 168 us -> 163 us (0.970)
  the two profiles are of different devices: /device:TPU:1 before, /device:TPU:206 now
where the time goes in v3:
time: 163 us
  Pallas kernels  162 us (99%)
    pallas_call x1, Pallas kernels, exchange(): pl.pallas_call(exchange_kernel, out_shape=[jax.ShapeDtypeStruct((4, SLOTS...  136 us
    pallas_call x1, Pallas kernels, attend(): pl.pallas_call(attend_kernel, out_shape=jax.ShapeDtypeStruct((SLOTS, 4 *...  25.8 us

profile of v3, /device:TPU:206, one launch (start us, length us, event | category | flops | bytes accessed | tf_op | source)
XLA Modules:
  0.0 162.5 jit_solution(4086360501055602929)
XLA Ops:
  0.7 136.1 %shard_map.100 = (bf16[4,512,128]{2,1,0:T(8,128)(2,1)}, bf16[512,256]{1,0:T(8,128)(2,1)}, bf16[32,192,256]{2,1,0:T(8,128)(2,1)}) custom-call(bf16[512,1024]{1,0:T(8,128)(2,1)} %hidden.1, bf16[8192]{0:T(1024)(128)(2,1)} %gain.1, bf16[256,512]{1,0:T(8,128)(2,1)} %wq.1, bf16[256,128]{1,0:T(8,128)(2,1)} %km.1, bf16[256,128]{1,0:T(8,128)(2,1)} %vm.1, ...), custom_call_target="tpu_custom_call" | custom-call | tf_op jit(solution)/shard_map/pallas_call | solution.py:392
  136.8 25.8 %shard_map.101 = bf16[512,512]{1,0:T(8,128)(2,1)} custom-call(s32[1,6]{1,0:T(1,128)} %ids.3, s32[128]{0:T(128)} %placement.1, s32[1,4]{1,0:T(1,128)} %tiles.3, s32[1]{0:T(128)S(6)} %copy.11.count, bf16[4,512,128]{2,1,0:T(8,128)(2,1)} %get-tuple-element.8.q, bf16[512,256]{1,0:T(8,128)(2,1)} %get-tuple-element.9.kv, bf16[32,192,256]{2,1,0:T(8,128)(2,1)} %get-tuple-element.10.inbox), custom_call_target="tpu_custom_call" | custom-call | tf_op jit(solution)/shard_map/pallas_call | solution.py:522
